TPU v7x, 32 devices: a whole 2x2x4 slice. The times are simulated.
32 devices in a mesh: grp: 4 (over z), dev: 8 (over y, x, core).
Axes of the slice: x: 2, y: 2, z: 4, core: 2. Of those that a mesh axis runs over, the one named last changes fastest.
Arguments:
- amplitudes: bfloat16 [1024, 589824], P('dev', 'grp'), may hold values from -6 to 6
- singles: float32 [32, 768], replicated, may hold values from -5 to 5
- pair_source: int32 [1024], replicated, may hold values from 0 to 1023, each once
- integrals: bfloat16 [589824, 512], P(('grp', 'dev')), may hold values from -0.0078125 to 0.0078125
Outputs:
- ladder: float32 [1024, 512], P('dev')
Inputs may be any that keep to these rules, and one draw needn't show every extreme that they name: `pair_source`: each occupied pair appears exactly once.
All inputs are finite; a program needn't handle non-finite values.
Results may differ from a plain program's by a relative error of at most 0.0029.
Values may be sent and summed in bfloat16 or wider, within the bound.
A program may use at most 320 MiB of HBM per device.

v0:
```python
import jax
import jax.numpy as jnp
from jax import lax
from jax.sharding import PartitionSpec as P


def body(amplitudes, singles, pair_source, integrals):
    local = lax.all_to_all(amplitudes, "dev", split_axis=1, concat_axis=0, tiled=True)
    occupied = singles.shape[0]
    virtual = singles.shape[1]
    count = local.shape[1]
    first = (lax.axis_index("grp") * lax.axis_size("dev") + lax.axis_index("dev")) * count
    cd_index = first + jnp.arange(count, dtype=jnp.int32)
    c_part = cd_index // virtual
    d_part = cd_index % virtual
    labels = jnp.arange(virtual, dtype=jnp.int32)[:, None]
    pick_c = (labels == c_part[None, :]).astype(jnp.float32)
    pick_d = (labels == d_part[None, :]).astype(jnp.float32)
    left_factor = jnp.dot(
        singles, pick_c, precision=lax.Precision.HIGHEST, preferred_element_type=jnp.float32
    )
    right_factor = jnp.dot(
        singles, pick_d, precision=lax.Precision.HIGHEST, preferred_element_type=jnp.float32
    )
    dressing = (left_factor[:, None, :] * right_factor[None, :, :]).reshape(
        occupied * occupied, count
    )
    ordered = jnp.take(local, pair_source, axis=0)
    tau = (ordered.astype(jnp.float32) + dressing).astype(jnp.bfloat16)
    share = occupied * occupied // lax.axis_size("dev")
    partial_value = jnp.dot(tau, integrals, preferred_element_type=jnp.float32)
    summed = lax.psum(partial_value, ("grp", "dev"))
    return lax.dynamic_slice_in_dim(summed, lax.axis_index("dev") * share, share, 0)


def solution(mesh):
    placed = (P("dev", "grp"), P(), P(), P(("grp", "dev"), None))
    return jax.shard_map(
        body, mesh=mesh, in_specs=placed, out_specs=P("dev", None), check_vma=False
    )
```

profile of v0, /device:TPU:0, one launch (start us, length us, event | category | flops | bytes accessed | tf_op | source)
XLA Modules:
  0.0 772.0 jit_solution(15173130806688675399)
XLA Ops:
  6.5 0.0 copy-start
  6.5 25.5 %copy.8 = bf16[16,8,8,18432]{3,2,0,1:T(8,128)(2,1)} copy(bf16[16,8,8,18432]{3,2,1,0:T(8,128)(2,1)} %bitcast.20) | data formatting | bytes 75497472 | tf_op jit(solution)/shard_map/all_to_all | solution.py:8
  32.0 0.0 copy-start.2
  32.0 7.7 all-to-all-start
  39.7 0.0 all-reduce.2.cloned.1.call-start
  39.8 0.0 copy-done.2
  39.8 0.1 add_select_fusion
  39.9 0.0 copy-done
  39.9 20.2 %fusion.5 = f32[32,18432]{1,0:T(8,128)S(1)} fusion(f32[32,768]{1,0:T(8,128)S(1)} %copy-done, s32[18432]{0:T(1024)S(1)} %get-tuple-element.5), kind=kOutput, calls=%fused_computation.11 | convolution fusion | flops 5449973760 | bytes 2531328 | tf_op jit(solution)/shard_map/dot_general | solution.py:22
  60.1 21.7 %fusion.6 = f32[32,18432]{1,0:T(8,128)} fusion(f32[32,768]{1,0:T(8,128)S(1)} %copy-done, s32[18432]{0:T(1024)S(1)} %get-tuple-element.6), kind=kOutput, calls=%fused_computation.12 | convolution fusion | flops 5449973760 | bytes 2531328 | tf_op jit(solution)/shard_map/dot_general | solution.py:19
  81.8 25.2 %broadcast_multiply_fusion = f32[32,32,18432]{2,1,0:T(8,128)} fusion(f32[32,18432]{1,0:T(8,128)S(1)} %fusion.5, f32[32,18432]{1,0:T(8,128)} %fusion.6), kind=kLoop, calls=%fused_computation.8 | loop fusion | flops 18874368 | bytes 80216064 | tf_op jit(solution)/shard_map/mul | solution.py:25
  107.0 341.9 %all-to-all-done = bf16[128,8,18432]{2,0,1:T(8,128)(2,1)} async-done(((bf16[128,8,18432]{2,0,1:T(8,128)(2,1)}), bf16[128,8,18432]{2,0,1:T(8,128)(2,1)}, u32[]{:S(2)}, u32[]{:S(2)}) %all-to-all-start) | async-done | bytes 37748768 | tf_op jit(solution)/shard_map/all_to_all | solution.py:8
  448.9 104.1 %gather_fusion = bf16[1024,18432]{1,0:T(8,128)(2,1)} fusion(bf16[1024,18432]{1,0:T(8,128)(2,1)} %bitcast.1, s32[1024]{0:T(1024)S(1)} %fusion.12), kind=kCustom, calls=%fused_computation | custom fusion | bytes 75501568 | tf_op jit(solution)/shard_map/jit(_take)/gather | solution.py:28
  553.0 0.0 copy-start.1
  553.0 47.7 %fusion = bf16[1024,18432]{1,0:T(8,128)(2,1)} fusion(f32[32,32,18432]{2,1,0:T(8,128)} %broadcast_multiply_fusion, bf16[1024,18432]{1,0:T(8,128)(2,1)} %gather_fusion, pred[1024]{0:T(1024)(128)(4,1)S(1)} %compare_and_fusion), kind=kLoop, calls=%fused_computation.2 | loop fusion | flops 75497472 | bytes 150995968 | tf_op jit(solution)/shard_map/convert_element_type | solution.py:29
  600.7 28.1 %fusion.13 = f32[1024,512]{1,0:T(8,128)} fusion(bf16[1024,18432]{1,0:T(8,128)(2,1)} %fusion, bf16[18432,512]{1,0:T(8,128)(2,1)} %param.7), kind=kOutput, calls=%fused_computation.26 | convolution fusion | flops 19327352832 | bytes 58720256 | tf_op jit(solution)/shard_map/dot_general | solution.py:31
  628.8 0.0 all-reduce.2.cloned.1.call-update
  628.8 134.3 %all-reduce.2.cloned.1.call-done = f32[1024,512]{1,0:T(8,128)} async-done(((f32[1024,512]{1,0:T(8,128)}), f32[1024,512]{1,0:T(8,128)}) %all-reduce.2.cloned.1.call-update) | async-done | bytes 2097168 | tf_op jit(solution)/shard_map/psum | solution.py:32
  763.0 1.7 constant_dynamic-slice_fusion
  764.7 0.0 copy-done.1
  (2 shorter events, 0.0 us)
Async XLA Ops:
  6.5 33.3 %copy-start = (f32[32,768]{1,0:T(8,128)S(1)}, f32[32,768]{1,0:T(8,128)}, u32[]{:S(2)}) copy-start(f32[32,768]{1,0:T(8,128)} %param.5) | copy-start | bytes 294916
  32.0 7.7 %copy-start.2 = (s32[1024]{0:T(1024)S(1)}, s32[1024]{0:T(1024)}, u32[]{:S(2)}) copy-start(s32[1024]{0:T(1024)} %param.6) | copy-start | bytes 12292
  32.0 416.9 %all-to-all-start = ((bf16[128,8,18432]{2,0,1:T(8,128)(2,1)}), bf16[128,8,18432]{2,0,1:T(8,128)(2,1)}, u32[]{:S(2)}, u32[]{:S(2)}) async-start(bf16[128,8,18432]{2,0,1:T(8,128)(2,1)} %bitcast.19), calls=%async_computation | async-start | bytes 75497472 | tf_op jit(solution)/shard_map/all_to_all | solution.py:8
  39.7 723.3 %all-reduce.2.cloned.1.call-start = ((), (), s32[]{:S(2)}) async-start(), calls=%async_computation.1 | async-start | bytes 4194304 | tf_op jit(solution)/shard_map/psum | solution.py:32
  553.0 211.7 %copy-start.1 = (f32[32,768]{1,0:T(8,128)S(1)}, f32[32,768]{1,0:T(8,128)}, u32[]{:S(2)}) copy-start(f32[32,768]{1,0:T(8,128)} %param.5) | copy-start | bytes 294916
Sparse Core Ops, SparseCore 0:
  628.9 134.0 all-reduce.1
where the time goes:
time: 781 us; the launch traced here: 772 us
  waiting for transfers between devices  476 us (61%)
  local copies, waits for them, and re-layouts  131 us (17%)
  other arithmetic  73 us (9%)
  matrix products  70 us (9%)
  between operations  13.9 us (2%)
    all_to_all x1, waiting for transfers between devices, body(): lax.all_to_all(amplitudes, 'dev', split_axis=1, concat_axis=0, tiled=True)  342 us
    psum x1, waiting for transfers between devices, body(): summed = lax.psum(partial_value, ('grp', 'dev'))  134 us
    gather x1, local copies, waits for them, and re-layouts, body(): ordered = jnp.take(local, pair_source, axis=0)  104 us
    convert_element_type x1, other arithmetic, body(): tau = (ordered.astype(jnp.float32) + dressing).astype(jnp.bfloat16)  47.7 us
    dot_general x1, matrix products, body(): partial_value = jnp.dot(tau, integrals, preferred_element_type=jnp.float32)  28.1 us
    all_to_all x1, local copies, waits for them, and re-layouts, body(): lax.all_to_all(amplitudes, 'dev', split_axis=1, concat_axis=0, tiled=True)  25.5 us
    mul x1, other arithmetic, body(): left_factor[:, None, :] * right_factor[None, :, :]  25.2 us
    dot_general x1, matrix products, body(): jnp.dot(singles, pick_c, precision=lax.Precision.HIGHEST, preferred_eleme...  21.7 us
  transfers between devices with their start and end apart: 2, of which 2 were waited for; matrix products, arithmetic and copies ran while one was open for 9% of the time, Pallas kernels for 0%

commit v1 on v0

--- a/solution.py
+++ b/solution.py
@@ -29,7 +29,7 @@
     tau = (ordered.astype(jnp.float32) + dressing).astype(jnp.bfloat16)
     share = occupied * occupied // lax.axis_size("dev")
     partial_value = jnp.dot(tau, integrals, preferred_element_type=jnp.float32)
-    summed = lax.psum(partial_value, ("grp", "dev"))
+    summed = jnp.sum(lax.all_gather(partial_value, ("grp", "dev")), axis=0)
     return lax.dynamic_slice_in_dim(summed, lax.axis_index("dev") * share, share, 0)
 
 

time: 781 us -> 1020 us (1.31)
  waiting for transfers between devices: 476 us -> 699 us
  other arithmetic: 73 us -> 93.9 us
    all_gather x0 -> x1, waiting for transfers between devices: none -> 357 us  [body(): summed = jnp.sum(lax.all_gather(partial_value, ('grp', 'dev')), axis=0)]
    psum x1 -> x0, waiting for transfers between devices: 134 us -> none  [body(): summed = lax.psum(partial_value, ('grp', 'dev'))]
    reduce_sum x0 -> x1, other arithmetic: none -> 20.9 us  [body(): summed = jnp.sum(lax.all_gather(partial_value, ('grp', 'dev')), axis=0)]
  transfers between devices with their start and end apart: 2 -> 2, of which waited for: 2 -> 2; matrix products, arithmetic and copies ran while one was open for 9% -> 7% of each run, Pallas kernels for 0% -> 0%
where the time goes in v1:
time: 1020 us; the launch traced here: 1010 us
  waiting for transfers between devices  699 us (69%)
  local copies, waits for them, and re-layouts  130 us (13%)
  other arithmetic  93.9 us (9%)
  matrix products  69.9 us (7%)
  between operations  13.9 us (1%)
    all_gather x1, waiting for transfers between devices, body(): summed = jnp.sum(lax.all_gather(partial_value, ('grp', 'dev')), axis=0)  357 us
    all_to_all x1, waiting for transfers between devices, body(): lax.all_to_all(amplitudes, 'dev', split_axis=1, concat_axis=0, tiled=True)  342 us
    gather x1, local copies, waits for them, and re-layouts, body(): ordered = jnp.take(local, pair_source, axis=0)  104 us
    convert_element_type x1, other arithmetic, body(): tau = (ordered.astype(jnp.float32) + dressing).astype(jnp.bfloat16)  47.7 us
    dot_general x1, matrix products, body(): partial_value = jnp.dot(tau, integrals, preferred_element_type=jnp.float32)  28 us
    all_to_all x1, local copies, waits for them, and re-layouts, body(): lax.all_to_all(amplitudes, 'dev', split_axis=1, concat_axis=0, tiled=True)  25.5 us
    mul x1, other arithmetic, body(): left_factor[:, None, :] * right_factor[None, :, :]  25.2 us
    dot_general x1, matrix products, body(): jnp.dot(singles, pick_c, precision=lax.Precision.HIGHEST, preferred_eleme...  21.7 us
  transfers between devices with their start and end apart: 2, of which 2 were waited for; matrix products, arithmetic and copies ran while one was open for 7% of the time, Pallas kernels for 0%

profile of v1, /device:TPU:0, one launch (start us, length us, event | category | flops | bytes accessed | tf_op | source)
XLA Modules:
  0.0 1014.4 jit_solution(2865754621683897523)
XLA Ops:
  6.5 0.0 copy-start
  6.5 25.5 %copy.8 = bf16[16,8,8,18432]{3,2,0,1:T(8,128)(2,1)} copy(bf16[16,8,8,18432]{3,2,1,0:T(8,128)(2,1)} %bitcast.21) | data formatting | bytes 75497472 | tf_op jit(solution)/shard_map/all_to_all | solution.py:8
  32.0 0.0 copy-start.2
  32.0 7.7 all-to-all-start
  39.7 0.0 all-gather.3.cloned.1.call-start
  39.8 0.0 copy-done.2
  39.8 0.1 add_select_fusion
  39.9 0.0 copy-done
  39.9 20.2 %fusion.5 = f32[32,18432]{1,0:T(8,128)S(1)} fusion(f32[32,768]{1,0:T(8,128)S(1)} %copy-done, s32[18432]{0:T(1024)S(1)} %get-tuple-element.5), kind=kOutput, calls=%fused_computation.11 | convolution fusion | flops 5449973760 | bytes 2531328 | tf_op jit(solution)/shard_map/dot_general | solution.py:22
  60.1 21.7 %fusion.6 = f32[32,18432]{1,0:T(8,128)} fusion(f32[32,768]{1,0:T(8,128)S(1)} %copy-done, s32[18432]{0:T(1024)S(1)} %get-tuple-element.6), kind=kOutput, calls=%fused_computation.12 | convolution fusion | flops 5449973760 | bytes 2531328 | tf_op jit(solution)/shard_map/dot_general | solution.py:19
  81.8 25.2 %broadcast_multiply_fusion = f32[32,32,18432]{2,1,0:T(8,128)} fusion(f32[32,18432]{1,0:T(8,128)S(1)} %fusion.5, f32[32,18432]{1,0:T(8,128)} %fusion.6), kind=kLoop, calls=%fused_computation.8 | loop fusion | flops 18874368 | bytes 80216064 | tf_op jit(solution)/shard_map/mul | solution.py:25
  107.0 341.9 %all-to-all-done = bf16[128,8,18432]{2,0,1:T(8,128)(2,1)} async-done(((bf16[128,8,18432]{2,0,1:T(8,128)(2,1)}), bf16[128,8,18432]{2,0,1:T(8,128)(2,1)}, u32[]{:S(2)}, u32[]{:S(2)}) %all-to-all-start) | async-done | bytes 37748768 | tf_op jit(solution)/shard_map/all_to_all | solution.py:8
  448.9 104.1 %gather_fusion = bf16[1024,18432]{1,0:T(8,128)(2,1)} fusion(bf16[1024,18432]{1,0:T(8,128)(2,1)} %bitcast.1, s32[1024]{0:T(1024)S(1)} %fusion.12), kind=kCustom, calls=%fused_computation | custom fusion | bytes 75501568 | tf_op jit(solution)/shard_map/jit(_take)/gather | solution.py:28
  553.0 47.7 %fusion = bf16[1024,18432]{1,0:T(8,128)(2,1)} fusion(f32[32,32,18432]{2,1,0:T(8,128)} %broadcast_multiply_fusion, bf16[1024,18432]{1,0:T(8,128)(2,1)} %gather_fusion, pred[1024]{0:T(1024)(128)(4,1)S(1)} %compare_and_fusion), kind=kLoop, calls=%fused_computation.2 | loop fusion | flops 75497472 | bytes 150995968 | tf_op jit(solution)/shard_map/convert_element_type | solution.py:29
  600.6 0.0 copy-start.1
  600.7 28.0 %fusion.13 = f32[1024,512]{1,0:T(8,128)} fusion(bf16[1024,18432]{1,0:T(8,128)(2,1)} %fusion, bf16[18432,512]{1,0:T(8,128)(2,1)} %param.7), kind=kOutput, calls=%fused_computation.26 | convolution fusion | flops 19327352832 | bytes 58720256 | tf_op jit(solution)/shard_map/dot_general | solution.py:31
  628.7 0.0 all-gather.3.cloned.1.call-update
  628.7 356.7 %all-gather.3.cloned.1.call-done = f32[32768,512]{1,0:T(8,128)} async-done(((f32[1024,512]{1,0:T(8,128)}), f32[32768,512]{1,0:T(8,128)}) %all-gather.3.cloned.1.call-update) | async-done | bytes 67108880 | tf_op jit(solution)/shard_map/all_gather | solution.py:32
  985.4 20.9 %reduce_sum.9 = f32[1024,512]{1,0:T(8,128)S(1)} reduce(f32[32,1024,512]{2,1,0:T(8,128)} %bitcast.5, f32[]{:T(128)} %constant.51.clone.1), dimensions={0}, to_apply=%region_0.1 | reduce | flops 16252928 | bytes 69206016 | tf_op jit(solution)/shard_map/reduce_sum | solution.py:32
  1006.3 0.7 constant_dynamic-slice_fusion
  1007.1 0.0 copy-done.1
  (2 shorter events, 0.0 us)
Async XLA Ops:
  6.5 33.3 %copy-start = (f32[32,768]{1,0:T(8,128)S(1)}, f32[32,768]{1,0:T(8,128)}, u32[]{:S(2)}) copy-start(f32[32,768]{1,0:T(8,128)} %param.5) | copy-start | bytes 294916
  32.0 7.7 copy-start.2
  32.0 416.9 %all-to-all-start = ((bf16[128,8,18432]{2,0,1:T(8,128)(2,1)}), bf16[128,8,18432]{2,0,1:T(8,128)(2,1)}, u32[]{:S(2)}, u32[]{:S(2)}) async-start(bf16[128,8,18432]{2,0,1:T(8,128)(2,1)} %bitcast.20), calls=%async_computation | async-start | bytes 75497472 | tf_op jit(solution)/shard_map/all_to_all | solution.py:8
  39.7 945.7 %all-gather.3.cloned.1.call-start = ((), (), s32[]{:S(2)}) async-start(), calls=%async_computation.1 | async-start | bytes 69206016 | tf_op jit(solution)/shard_map/all_gather | solution.py:32
  600.6 406.4 %copy-start.1 = (f32[32,768]{1,0:T(8,128)S(1)}, f32[32,768]{1,0:T(8,128)}, u32[]{:S(2)}) copy-start(f32[32,768]{1,0:T(8,128)} %param.5) | copy-start | bytes 294916
Sparse Core Ops, SparseCore 0:
  628.8 356.5 all-gather.2
